TPU v7x, 32 devices: a whole 2x2x4 slice. The times are simulated.
32 devices in a mesh: clips: 2 (over x), pix: 2 (over core), frame: 8 (over z, y).
Axes of the slice: x: 2, y: 2, z: 4, core: 2. Of those that a mesh axis runs over, the one named last changes fastest.
Arguments:
- stream: bfloat16 [2, 16, 384, 1152], P(None, ('clips', 'frame'), 'pix'), parts along dimension 1, may hold values from -8 to 8
- spatial_qkv: bfloat16 [2, 3, 16, 384, 1152], P(None, None, ('clips', 'frame'), 'pix'), parts along dimension 2, as said below
- out_weight: bfloat16 [1152, 1152], P(None, 'frame'), may hold values from -0.1875 to 0.1875
- qkv_weight: bfloat16 [1152, 3456], P(None, 'frame')
- mod_table: float32 [3, 2, 1152], replicated, may hold values from -3 to 3
- timestep: int32 [2], P('clips'), parts along dimension 0, may hold values from 0 to 999
Outputs:
- residual: float32 [2, 16, 384, 1152], P(None, ('clips', 'frame'), 'pix'), parts along dimension 1
- temporal: float32 [2, 16, 384, 1152], P(None, ('clips', 'frame'), 'pix'), parts along dimension 1
There are 2 independent parts, one for each index of `clips`. A program takes and returns all parts, laid end to end along the dimension named above; an argument that names none is the same for every part. Nothing has to cross between parts.
Inputs may be any that keep to these rules, and one draw needn't show every extreme that they name: `spatial_qkv`: Queries, keys and values of the spatial attention, primal in the first index and tangent in the second.
All inputs are finite; a program needn't handle non-finite values.
Results may differ from a plain program's by a relative error of at most 0.0097.
Values may be sent and summed in bfloat16 or wider, within the bound.
A program may use at most 128 MiB of HBM per device.

v0:
```python
import math

import jax
import jax.numpy as jnp
from jax import lax
from jax.sharding import PartitionSpec as P

HEAD_DIM = 72


def modulation(mod_table, timestep):
    width = mod_table.shape[-1]
    frequency = jnp.exp(-math.log(10.0) * jnp.arange(width).astype(jnp.float32) / width)
    time_value = timestep[0].astype(jnp.float32) * (math.pi / 1000.0)
    mod_value = mod_table[:, 0] + mod_table[:, 1] * jnp.cos(frequency * time_value)
    mod_slope = -mod_table[:, 1] * frequency * jnp.sin(frequency * time_value)
    return (mod_value, mod_slope)


def attend_group(inputs):
    query, keys, values, query_dot, keys_dot, values_dot = inputs
    scale = 1.0 / math.sqrt(query.shape[-1])
    scores = jnp.einsum("blhe,bmhe->bhlm", query, keys, preferred_element_type=jnp.float32) * scale
    scores_dot = (
        jnp.einsum("blhe,bmhe->bhlm", query_dot, keys, preferred_element_type=jnp.float32)
        + jnp.einsum("blhe,bmhe->bhlm", query, keys_dot, preferred_element_type=jnp.float32)
    ) * scale
    top_score = jnp.max(scores, axis=-1, keepdims=True)
    expo = jnp.exp(scores - top_score)
    probs = expo / jnp.sum(expo, axis=-1, keepdims=True)
    probs_low = probs.astype(jnp.bfloat16)
    output = jnp.einsum("bhlm,bmhe->blhe", probs_low, values, preferred_element_type=jnp.float32)
    row_total = jnp.sum(probs * scores_dot, axis=-1, keepdims=True)
    weighted = probs * (scores_dot - row_total)
    weighted_low = weighted.astype(jnp.bfloat16)
    output_dot = jnp.einsum(
        "bhlm,bmhe->blhe", weighted_low, values, preferred_element_type=jnp.float32
    ) + jnp.einsum("bhlm,bmhe->blhe", probs_low, values_dot, preferred_element_type=jnp.float32)
    return (output, output_dot)


def attend(stacked, group_size):
    batch, length, heads_all, head_size = stacked.shape[2:]
    groups = heads_all // group_size
    shaped = stacked.reshape(2, 3, batch, length, groups, group_size, head_size)
    shaped = jnp.transpose(shaped, (4, 0, 1, 2, 3, 5, 6))
    inputs = (
        shaped[:, 0, 0],
        shaped[:, 0, 1],
        shaped[:, 0, 2],
        shaped[:, 1, 0],
        shaped[:, 1, 1],
        shaped[:, 1, 2],
    )
    output, output_dot = lax.map(attend_group, inputs)
    joined = jnp.stack([output, output_dot], axis=1)
    joined = jnp.transpose(joined, (1, 2, 3, 0, 4, 5))
    return joined.reshape(2, batch, length, heads_all * head_size)


def per_device(stream, spatial_qkv, out_weight, qkv_weight, mod_table, timestep):
    frames_local = stream.shape[1]
    places = stream.shape[2]
    width = stream.shape[3]
    block = lax.all_to_all(spatial_qkv, "pix", split_axis=4, concat_axis=3, tiled=True)
    frames_here = block.shape[2]
    length = block.shape[3]
    channels = block.shape[4]
    shaped = block.reshape(2, 3, frames_here, length, channels // HEAD_DIM, HEAD_DIM)
    attended = attend(shaped, 1).astype(jnp.bfloat16)
    spatial = lax.all_to_all(attended, "pix", split_axis=2, concat_axis=3, tiled=True)
    flat_spatial = spatial.reshape(-1, width)
    projected = jnp.dot(
        flat_spatial,
        lax.all_gather(out_weight, "frame", axis=1, tiled=True),
        preferred_element_type=jnp.float32,
    )
    projected = projected.reshape(2, frames_local, places, width)
    mod_value, mod_slope = modulation(mod_table, timestep)
    primal_in = stream[0].astype(jnp.float32)
    tangent_in = stream[1].astype(jnp.float32)
    hidden = primal_in + mod_value[0] * projected[0]
    hidden_dot = tangent_in + mod_slope[0] * projected[0] + mod_value[0] * projected[1]
    centered = hidden - jnp.mean(hidden, axis=-1, keepdims=True)
    inv_scale = lax.rsqrt(jnp.mean(centered * centered, axis=-1, keepdims=True) + 1e-06)
    normed = centered * inv_scale
    normed_dot = (
        hidden_dot
        - jnp.mean(hidden_dot, axis=-1, keepdims=True)
        - normed * jnp.mean(normed * hidden_dot, axis=-1, keepdims=True)
    ) * inv_scale
    modulated = normed * (1.0 + mod_value[2]) + mod_value[1]
    modulated_dot = normed_dot * (1.0 + mod_value[2]) + normed * mod_slope[2] + mod_slope[1]
    modulated_low = jnp.stack([modulated, modulated_dot]).astype(jnp.bfloat16)
    moved_rows = lax.all_to_all(modulated_low, "frame", split_axis=2, concat_axis=1, tiled=True)
    frames_all = moved_rows.shape[1]
    sub_places = moved_rows.shape[2]
    flat_rows = moved_rows.reshape(-1, width)
    projected_qkv = (
        jnp.dot(
            flat_rows,
            lax.all_gather(qkv_weight, "frame", axis=1, tiled=True),
            preferred_element_type=jnp.float32,
        )
        .astype(jnp.bfloat16)
        .reshape(2, frames_all, sub_places, 3, width)
    )
    moved = jnp.transpose(projected_qkv, (0, 3, 1, 2, 4))
    frames_all = moved.shape[2]
    sub_places = moved.shape[3]
    arranged = jnp.transpose(moved, (0, 1, 3, 2, 4)).reshape(
        2, 3, sub_places, frames_all, width // HEAD_DIM, HEAD_DIM
    )
    attended = attend(arranged, width // HEAD_DIM)
    attended = jnp.transpose(attended, (0, 2, 1, 3))
    temporal = lax.all_to_all(attended, "frame", split_axis=1, concat_axis=2, tiled=True)
    residual = jnp.stack([hidden, hidden_dot])
    return (residual, temporal)


def solution(mesh):
    in_specs = (
        P(None, ("clips", "frame"), "pix", None),
        P(None, None, ("clips", "frame"), "pix", None),
        P(None, "frame"),
        P(None, "frame"),
        P(),
        P("clips"),
    )
    out_specs = (P(None, ("clips", "frame"), "pix", None), P(None, ("clips", "frame"), "pix", None))
    return jax.shard_map(
        per_device, mesh=mesh, in_specs=in_specs, out_specs=out_specs, check_vma=False
    )
```

profile of v0, /device:TPU:0, one launch (start us, length us, event | category | flops | bytes accessed | tf_op | source)
XLA Modules:
  0.0 311.3 jit_solution(2216087324205465143)
XLA Ops:
  7.2 0.7 all-gather.3.cloned.1.call-update
  7.9 8.4 %copy.101 = bf16[2,3,1,192,1152]{3,1,2,0,4:T(4,128)(2,1)} copy(bf16[2,3,1,192,1152]{4,3,2,1,0:T(8,128)(2,1)} %param.9) | data formatting | bytes 5308416 | tf_op args[1]
  16.3 5.8 %all-to-all-start = ((bf16[2,3,1,192,1152]{3,1,2,0,4:T(4,128)(2,1)}), bf16[2,3,1,192,1152]{3,1,2,0,4:T(4,128)(2,1)}, u32[]{:S(2)}, u32[]{:S(2)}) async-start(bf16[2,3,1,192,1152]{3,1,2,0,4:T(4,128)(2,1)} %copy.101), calls=%async_computation | async-start | bytes 9437184 | tf_op jit(solution)/shard_map/all_to_all | solution.py:65
  22.2 0.7 all-gather.5.cloned.1.call-update
  22.9 4.1 %all-to-all-done = bf16[2,3,1,192,1152]{3,1,2,0,4:T(4,128)(2,1)} async-done(((bf16[2,3,1,192,1152]{3,1,2,0,4:T(4,128)(2,1)}), bf16[2,3,1,192,1152]{3,1,2,0,4:T(4,128)(2,1)}, u32[]{:S(2)}, u32[]{:S(2)}) %all-to-all-start) | async-done | bytes 2654240 | tf_op jit(solution)/shard_map/all_to_all | solution.py:65
  27.0 6.6 %copy.184 = bf16[2,3,1,192,2,576]{3,4,5,1,0,2:T(2,128)(2,1)S(1)} copy(bf16[2,3,1,192,2,576]{3,1,0,5,4,2:T(4,128)(2,1)} %bitcast.15) | data formatting | bytes 5308416 | tf_op jit(solution)/shard_map/all_to_all | solution.py:65
  33.6 3.1 %reshape_reshape.3 = bf16[2,3,1,384,8,1,72]{3,6,4,1,0,5,2:T(8,128)(2,1)} reshape(bf16[2,3,1,2,192,576]{4,3,5,1,0,2:T(2,128)(2,1)S(1)} %bitcast.197) | data formatting | bytes 5308416 | tf_op jit(solution)/shard_map/reshape;reshape | solution.py:45
  36.8 2.0 slice_bitcast_fusion
  38.8 15.0 %while.2 = (s32[]{:T(128)}, bf16[8,1,384,1,72]{2,4,3,1,0:T(8,128)(2,1)S(1)}, bf16[8,1,384,1,72]{2,4,3,1,0:T(8,128)(2,1)S(1)}, bf16[8,1,384,1,72]{2,4,3,1,0:T(8,1...) while((s32[]{:T(128)}, ...), condition=%wide.region_4.5_spmd, body=%wide.region_0.4_spmd.sunk | while | flops 130525056 | bytes 6868073 | solution.py:55
  38.8 0.3 fusion.89
  39.3 0.3 fusion.92
  39.6 0.3 multiply_reduce_fusion.5
  39.9 0.3 fusion.93
  40.7 0.3 fusion.89
  41.1 0.3 fusion.92
  41.4 0.3 multiply_reduce_fusion.5
  41.8 0.3 fusion.93
  42.6 0.3 fusion.89
  43.3 0.3 multiply_reduce_fusion.5
  43.6 0.3 fusion.93
  44.5 0.3 fusion.89
  44.9 0.3 fusion.92
  45.2 0.3 multiply_reduce_fusion.5
  45.5 0.3 fusion.93
  46.3 0.3 fusion.89
  47.0 0.3 multiply_reduce_fusion.5
  47.4 0.3 fusion.93
  48.2 0.3 fusion.89
  48.9 0.3 multiply_reduce_fusion.5
  49.3 0.3 fusion.93
  50.1 0.3 fusion.89
  50.8 0.3 multiply_reduce_fusion.5
  51.9 0.3 fusion.89
  52.7 0.3 multiply_reduce_fusion.5
  53.0 0.3 fusion.93
  54.0 1.7 copy.106
  55.7 4.5 %all_to_all.51 = bf16[2,1,384,576]{3,0,1,2:T(2,128)(2,1)S(1)} all-to-all(bf16[2,1,384,576]{3,0,1,2:T(2,128)(2,1)S(1)} %copy.106), channel_id=1, replica_groups=mesh['clips'=2,'pix'=2,'frame'=8] {'pix'}, dimensions={2} | all-to-all | bytes 1769472 | tf_op jit(solution)/shard_map/all_to_all | solution.py:71
  60.4 1.0 copy.108
  61.4 0.6 reshape.275
  62.9 5.0 %all-gather.3.cloned.1.call-done = bf16[1152,1152]{0,1:T(8,128)(2,1)} async-done(((bf16[1152,144]{0,1:T(8,128)(2,1)}), bf16[1152,1152]{0,1:T(8,128)(2,1)}) %all-gather.3.cloned.1.call-update) | async-done | bytes 2654224 | tf_op jit(solution)/shard_map/all_gather | solution.py:75
  67.9 3.2 %fusion.64 = f32[384,1152]{1,0:T(8,128)S(1)} fusion(bf16[384,1152]{1,0:T(8,128)(2,1)S(1)} %reshape.275, bf16[1152,1152]{0,1:T(8,128)(2,1)} %all-gather.3.cloned.1.call-done), kind=kOutput, calls=%fused_computation.118 | convolution fusion | flops 1019215872 | bytes 5308416 | tf_op jit(solution)/shard_map/dot_general | solution.py:73
  71.6 0.4 fusion.57
  72.1 0.5 fusion.45
  72.7 0.9 copy.109
  73.6 48.1 %all_to_all.52 = bf16[2,1,192,1152]{3,0,1,2:T(2,128)(2,1)S(1)} all-to-all(bf16[2,1,192,1152]{3,0,1,2:T(2,128)(2,1)S(1)} %copy.109), channel_id=1, replica_groups=mesh['clips'=2,'pix'=2,'frame'=8] {'frame'}, dimensions={2} | all-to-all | bytes 1769472 | tf_op jit(solution)/shard_map/all_to_all | solution.py:95
  121.8 84.0 %all-gather.5.cloned.1.call-done = bf16[1152,3456]{0,1:T(8,128)(2,1)} async-done(((bf16[1152,432]{0,1:T(8,128)(2,1)}), bf16[1152,3456]{0,1:T(8,128)(2,1)}) %all-gather.5.cloned.1.call-update) | async-done | bytes 7962640 | tf_op jit(solution)/shard_map/all_gather | solution.py:102
  205.8 9.3 %convolution_convert_fusion = bf16[384,3456]{1,0:T(8,128)(2,1)} fusion(bf16[384,1152]{1,0:T(8,128)(2,1)S(1)} %bitcast.204, bf16[1152,3456]{0,1:T(8,128)(2,1)} %all-gather.5.cloned.1.call-done), kind=kOutput, calls=%fused_computation.43 | convolution fusion | flops 3058974720 | bytes 11501568 | tf_op jit(solution)/shard_map/dot_general | solution.py:100
  215.1 6.3 %reshape.277 = bf16[2,8,24,3,1152]{4,3,2,1,0:T(4,128)(2,1)} reshape(bf16[384,3456]{1,0:T(8,128)(2,1)} %convolution_convert_fusion) | data formatting | bytes 5308416 | tf_op jit(solution)/shard_map/reshape | solution.py:106
  221.4 12.7 %reshape.280 = bf16[1,2,3,24,8,16,72]{6,5,2,3,4,1,0:T(8,128)(2,1)} reshape(bf16[2,3,24,8,1152]{4,1,2,3,0:T(4,128)(2,1)} %bitcast.198) | data formatting | bytes 5308416 | tf_op jit(solution)/shard_map/transpose;reshape;reshape | solution.py:46
  234.1 4.9 %fusion.61 = (bf16[1,1,1,24,8,16,72]{6,5,2,3,4,1,0:T(8,128)(2,1)}, bf16[1,1,1,24,8,16,72]{6,5,2,3,4,1,0:T(8,128)(2,1)}, bf16[1,1,1,24,8,16,72]{6,5,2,3,4,1,0:T(8...) fusion(bf16[1,2,3,24,8,16,72]{6,5,2,3,4,1,0:T(8,128)(2,1)} %res, ...), kind=kLoop, calls=%fused_computation.115 | loop fusion | bytes 5308416 | tf_op jit(solution)/shard_map/slice | solution.py:53
  239.0 4.5 %fusion.63 = (f32[24,16,8]{2,1,0:T(8,128)S(1)}, f32[24,16,8,8]{2,3,1,0:T(8,128)}) fusion(bf16[1,1,1,24,8,16,72]{6,5,2,3,4,1,0:T(8,128)(2,1)} %get-tuple-element.124, bf16[1,1,1,24,8,16,72]{6,5,2,3,4,1,0:T(8,128)(2,1)S(1)} %get-tuple-element.123), kind=kOutput, calls=%fused_computation.117 | convolution fusion | flops 3612679 | bytes 995328 | tf_op jit(solution)/shard_map/while/body/eval_jaxpr/sub | solution.py:29
  243.5 2.1 convolution_bitcast_fusion.1
  245.9 1.6 stack.48
  247.6 2.5 fusion.43
  250.1 1.5 multiply_reduce_fusion.1
  251.6 0.9 fusion.42
  252.8 0.8 add_bitcast_fusion
  253.9 1.6 stack.49
  255.5 1.5 maximum_bitcast_fusion
  257.0 1.5 copy.123
  258.6 3.6 %all-to-all-start.3 = ((f32[2,8,24,1152]{3,2,0,1:T(8,128)}), f32[2,8,24,1152]{3,2,0,1:T(8,128)S(1)}, u32[]{:S(2)}, u32[]{:S(2)}) async-start(f32[2,8,24,1152]{3,2,0,1:T(8,128)} %copy.123), calls=%async_computation.3 | async-start | bytes 3538944 | tf_op jit(solution)/shard_map/all_to_all | solution.py:116
  262.2 1.3 pad_maximum_fusion
  263.5 39.7 %all-to-all-done.3 = f32[2,8,24,1152]{3,2,0,1:T(8,128)S(1)} async-done(((f32[2,8,24,1152]{3,2,0,1:T(8,128)}), f32[2,8,24,1152]{3,2,0,1:T(8,128)S(1)}, u32[]{:S(2)}, u32[]{:S(2)}) %all-to-all-start.3) | async-done | bytes 1769504 | tf_op jit(solution)/shard_map/all_to_all | solution.py:116
  303.2 1.3 copy.124
  (75 shorter events, 8.6 us)
Async XLA Ops:
  7.2 60.8 %all-gather.3.cloned.1.call-start = ((), (), s32[]{:S(2)}) async-start(), calls=%async_computation.4 | async-start | bytes 2985984 | tf_op jit(solution)/shard_map/all_gather | solution.py:75
  16.3 10.7 %all-to-all-start = ((bf16[2,3,1,192,1152]{3,1,2,0,4:T(4,128)(2,1)}), bf16[2,3,1,192,1152]{3,1,2,0,4:T(4,128)(2,1)}, u32[]{:S(2)}, u32[]{:S(2)}) async-start(bf16[2,3,1,192,1152]{3,1,2,0,4:T(4,128)(2,1)} %copy.101), calls=%async_computation | async-start | bytes 9437184 | tf_op jit(solution)/shard_map/all_to_all | solution.py:65
  22.2 183.7 %all-gather.5.cloned.1.call-start = ((), (), s32[]{:S(2)}) async-start(), calls=%async_computation.5 | async-start | bytes 8957952 | tf_op jit(solution)/shard_map/all_gather | solution.py:102
  36.8 2.0 copy-start.7
  36.8 2.0 copy-start.8
  60.4 2.4 copy-start.9
  62.9 8.2 %copy-start.1 = (bf16[2,1,192,1152]{3,2,1,0:T(8,128)(2,1)S(1)}, bf16[2,1,192,1152]{3,2,1,0:T(8,128)(2,1)}, u32[]{:S(2)}) copy-start(bf16[2,1,192,1152]{3,2,1,0:T(8,128)(2,1)} %param.8) | copy-start | bytes 2654212
  239.0 4.5 %copy-start = (bf16[1,1,1,24,8,16,72]{6,5,2,3,4,1,0:T(8,128)(2,1)}, bf16[1,1,1,24,8,16,72]{6,5,2,3,4,1,0:T(8,128)(2,1)S(1)}, u32[]{:S(2)}) copy-start(bf16[1,1,1,24,8,16,72]{6,5,2,3,4,1,0:T(8,128)(2,1)S(1)} %get-tuple-element.123) | copy-start | bytes 1327108
  239.0 4.5 %copy-start.3 = (bf16[1,1,1,24,8,16,72]{6,5,2,3,4,1,0:T(8,128)(2,1)}, bf16[1,1,1,24,8,16,72]{6,5,2,3,4,1,0:T(8,128)(2,1)S(1)}, u32[]{:S(2)}) copy-start(bf16[1,1,1,24,8,16,72]{6,5,2,3,4,1,0:T(8,128)(2,1)S(1)} %get-tuple-element.125) | copy-start | bytes 1327108
  247.6 2.5 copy-start.5
  247.6 2.5 copy-start.6
  247.6 2.5 copy-start.10
  250.1 1.5 copy-start.4
  251.6 1.1 copy-start.2
  258.6 44.6 %all-to-all-start.3 = ((f32[2,8,24,1152]{3,2,0,1:T(8,128)}), f32[2,8,24,1152]{3,2,0,1:T(8,128)S(1)}, u32[]{:S(2)}, u32[]{:S(2)}) async-start(f32[2,8,24,1152]{3,2,0,1:T(8,128)} %copy.123), calls=%async_computation.3 | async-start | bytes 3538944 | tf_op jit(solution)/shard_map/all_to_all | solution.py:116
Sparse Core Ops, SparseCore 0:
  10.2 57.7 all-gather.2
  70.1 135.6 all-gather.4
where the time goes:
time: 313 us; the launch traced here: 311 us
  waiting for transfers between devices  134 us (43%)
  local copies, waits for them, and re-layouts  55.6 us (18%)
  blocking collectives  52.7 us (17%)
  matrix products  38.4 us (12%)
  between operations  15 us (5%)
  starting transfers between devices  9.5 us (3%)
  other arithmetic  5.64 us (2%)
    all_gather x1, waiting for transfers between devices, per_device(): lax.all_gather(qkv_weight, 'frame', axis=1, tiled=True)  84 us
    all_to_all x1, blocking collectives, per_device(): lax.all_to_all(modulated_low, 'frame', split_axis=2, concat_axis=1, tiled...  48.1 us
    all_to_all x1, waiting for transfers between devices, per_device(): lax.all_to_all(attended, 'frame', split_axis=1, concat_axis=2, tiled=True)  39.7 us
    another operation x1, local copies, waits for them, and re-layouts, attend(): shaped = jnp.transpose(shaped, (4, 0, 1, 2, 3, 5, 6))  12.7 us
    dot_general x1, matrix products, per_device(): jnp.dot(flat_rows, lax.all_gather(qkv_weight, 'frame', axis=1, tiled=True...  9.33 us
    unnamed x23, local copies, waits for them, and re-layouts  8.67 us
    all_to_all x1, local copies, waits for them, and re-layouts, per_device(): lax.all_to_all(spatial_qkv, 'pix', split_axis=4, concat_axis=3, tiled=True)  6.61 us
    reshape x1, local copies, waits for them, and re-layouts, per_device(): projected_qkv = jnp.dot(flat_rows, lax.all_gather(qkv_weight, 'frame', ax...  6.29 us
  transfers between devices with their start and end apart: 4, of which 4 were waited for; matrix products, arithmetic and copies ran while one was open for 15% of the time, Pallas kernels for 0%

commit v1 on v0

--- a/solution.py
+++ b/solution.py
@@ -1,11 +1,16 @@
+import functools
 import math
 
 import jax
 import jax.numpy as jnp
 from jax import lax
+from jax.experimental import pallas as pl
+from jax.experimental.pallas import tpu as pltpu
 from jax.sharding import PartitionSpec as P
 
 HEAD_DIM = 72
+LANES = 128
+TILE = 384
 
 
 def modulation(mod_table, timestep):
@@ -118,6 +123,382 @@
     return (residual, temporal)
 
 
+def lane_window(head):
+    low = head * HEAD_DIM // LANES * LANES
+    high = -(-(head * HEAD_DIM + HEAD_DIM) // LANES) * LANES
+    return low, high
+
+
+def head_mask(head, low, high):
+    lane = lax.broadcasted_iota(jnp.int32, (1, high - low), 1) + low
+    return (lane >= head * HEAD_DIM) & (lane < (head + 1) * HEAD_DIM)
+
+
+def across(left, right):
+    return lax.dot_general(left, right, (((1,), (1,)), ((), ())), preferred_element_type=jnp.float32)
+
+
+def attend_head(mask, query, keys, values, query_dot, keys_dot, values_dot, allowed=None):
+    scale = 1.0 / math.sqrt(HEAD_DIM)
+    keep = mask.astype(jnp.float32).astype(jnp.bfloat16)
+    rows = query.shape[0]
+    query = query * keep
+    query_dot = query_dot * keep
+    both = across(jnp.concatenate([query, query_dot], axis=0), keys)
+    scores = both[:rows] * scale
+    scores_dot = (both[rows:] + across(query, keys_dot)) * scale
+    if allowed is not None:
+        scores = jnp.where(allowed, scores, -jnp.inf)
+    expo = jnp.exp(scores - jnp.max(scores, axis=-1, keepdims=True))
+    probs = expo * (1.0 / jnp.sum(expo, axis=-1, keepdims=True))
+    weighted = probs * (scores_dot - jnp.sum(probs * scores_dot, axis=-1, keepdims=True))
+    probs_low = probs.astype(jnp.bfloat16)
+    stacked = jnp.concatenate([probs_low, weighted.astype(jnp.bfloat16)], axis=0)
+    both = jnp.dot(stacked, values, preferred_element_type=jnp.float32)
+    output_dot = both[rows:] + jnp.dot(probs_low, values_dot, preferred_element_type=jnp.float32)
+    return both[:rows], output_dot
+
+
+class LaneTiles:
+    def __init__(self, heads):
+        self.held = {}
+        self.last = {}
+        for head in range(heads):
+            low, high = lane_window(head)
+            for tile in range(low // LANES, high // LANES):
+                self.last[tile] = head
+
+    def add(self, head, mask, output, output_dot):
+        low, high = lane_window(head)
+        done = []
+        for tile in range(low // LANES, high // LANES):
+            part = slice(tile * LANES - low, (tile + 1) * LANES - low)
+            here = mask[:, part]
+            pair = (output[:, part], output_dot[:, part])
+            if tile in self.held:
+                pair = tuple(jnp.where(here, a, b) for a, b in zip(pair, self.held[tile]))
+            self.held[tile] = pair
+            if self.last[tile] == head:
+                done.append((tile, self.held.pop(tile)))
+        return done
+
+
+def fused_kernel(
+    n, spatial, stream, out_own, qkv_own, mod, residual, returned,
+    peer_kv, out_all, qkv_all, attended, rows_send, rows_recv, qkv, back_send,
+    kv_sem, own_sem, ring_send, ring_recv, core_send, core_recv, x_send, x_recv,
+    xcore_send, xcore_recv, row_send_sem, row_recv_sem, back_send_sem, back_recv_sem,
+):
+    clip, core, me = lax.axis_index("clips"), lax.axis_index("pix"), lax.axis_index("frame")
+    side = lax.rem(clip, 2)
+    x_peer = clip + 1 - 2 * side
+    places, width = stream.shape[2], stream.shape[3]
+    part = places // n
+    heads = width // HEAD_DIM
+    half = n // 2
+
+    depth_of = lambda frame: lax.div(frame, 2)
+    row_of = lambda frame: lax.rem(frame, 2)
+    place_of = lambda frame: depth_of(frame) * (1 - row_of(frame)) + (n - 1 - depth_of(frame)) * row_of(frame)
+
+    def frame_at(place):
+        later = lax.div(place, half)
+        return (1 - later) * (2 * place) + later * (2 * (n - 1 - place) + 1)
+
+    place = place_of(me)
+    step_by = 1 - 2 * core
+    behind = lambda steps: frame_at(lax.rem(place - steps * step_by + 2 * n, n))
+    after = behind(-1)
+    to_peer = {"pix": 1 - core}
+    to_x = {"clips": x_peer}
+    to_next = {"frame": after}
+
+    barrier = pltpu.get_barrier_semaphore()
+    for target in [to_peer, to_x] + [{"frame": lax.rem(me + k, n)} for k in range(1, n)]:
+        pl.semaphore_signal(barrier, inc=1, device_id=target, device_id_type=pl.DeviceIdType.MESH)
+    pl.semaphore_wait(barrier, n + 1)
+
+    def remote(source, target, send, recv, device):
+        return pltpu.make_async_remote_copy(
+            src_ref=source, dst_ref=target, send_sem=send, recv_sem=recv,
+            device_id=device, device_id_type=pl.DeviceIdType.MESH,
+        )
+
+    kv_copy = remote(spatial.at[:, 1:3, 0], peer_kv, kv_sem.at[0], kv_sem.at[1], to_peer)
+    kv_copy.start()
+
+    gathered = (out_all, qkv_all)
+    owned = (out_own, qkv_own)
+    sizes = tuple(ref.shape[0] for ref in owned)
+    my_third = core + (1 - core) * 2 * side
+    peer_third = (1 - core) + core * 2 * side
+    x_third = 2 * (1 - side)
+
+    def piece(which, frame, third):
+        size = sizes[which] // 3
+        return gathered[which].at[pl.ds(pl.multiple_of(frame * sizes[which] + third * size, 16), size)]
+
+    def ring_copy(which, step):
+        block = piece(which, behind(step - 1), my_third)
+        if step == 1:
+            size = sizes[which] // 3
+            source = owned[which].at[pl.ds(pl.multiple_of(my_third * size, 16), size)]
+        else:
+            source = block
+        return remote(source, block, ring_send.at[which, step], ring_recv.at[which, step], to_next)
+
+    def arrives(block, recv):
+        return remote(block, block, kv_sem.at[0], recv, to_peer)
+
+    def core_copy(which, step):
+        block = piece(which, behind(step), my_third)
+        return remote(block, block, core_send.at[which, step], core_recv.at[which, step], to_peer)
+
+    def x_copy(which, step):
+        block = piece(which, behind(step), my_third)
+        return remote(block, block, x_send.at[which, step], x_recv.at[which, step], to_x)
+
+    def xcore_copy(which, step):
+        block = piece(which, behind(step), x_third)
+        return remote(block, block, xcore_send.at[which, step], xcore_recv.at[which, step], to_peer)
+
+    def ring_step(which, step):
+        arrives(piece(which, behind(step), my_third), ring_recv.at[which, step]).wait_recv()
+        if step < n - 1:
+            ring_copy(which, step + 1).start()
+
+        @pl.when(core == 0)
+        def _():
+            x_copy(which, step).start()
+
+        core_copy(which, step).start()
+
+    def x_step(which, step):
+        @pl.when(core == 0)
+        def _():
+            arrives(piece(which, behind(step), x_third), x_recv.at[which, step]).wait_recv()
+            xcore_copy(which, step).start()
+
+    def all_here(which):
+        for step in range(1, n):
+            other = frame_at(lax.rem(place + step * step_by + 2 * n, n))
+            arrives(piece(which, other, peer_third), core_recv.at[which, step]).wait_recv()
+
+        @pl.when(core == 1)
+        def _():
+            for step in range(1, n):
+                other = frame_at(lax.rem(place + step * step_by + 2 * n, n))
+                arrives(piece(which, other, x_third), xcore_recv.at[which, step]).wait_recv()
+
+    own_copies = []
+    for which in (0, 1):
+        ring_copy(which, 1).start()
+        whole = gathered[which].at[pl.ds(pl.multiple_of(me * sizes[which], 16), sizes[which])]
+        own_copies.append(pltpu.make_async_copy(owned[which], whole, own_sem.at[which]))
+        own_copies[-1].start()
+
+    events = []
+    for step in range(1, n):
+        events.append((2.0 * step, ring_step, 0, step))
+        events.append((2.0 * step + 2.0, x_step, 0, step))
+        events.append((4.0 * step, ring_step, 1, step))
+        events.append((4.0 * step + 3.0, x_step, 1, step))
+    events.sort(key=lambda event: event[0])
+
+    def serve(until):
+        while events and events[0][0] <= until:
+            _, act, which, step = events.pop(0)
+            act(which, step)
+
+    def serve_all(which):
+        for event in [event for event in events if event[2] == which]:
+            events.remove(event)
+            event[1](event[2], event[3])
+
+    kv_copy.wait_recv()
+    tiles = LaneTiles(heads)
+    for head in range(heads):
+        low, high = lane_window(head)
+        mask = head_mask(head, low, high)
+        both = lambda t, j: jnp.concatenate([spatial[t, 1 + j, 0, :, low:high], peer_kv[t, j, :, low:high]], axis=0)
+        output, output_dot = attend_head(
+            mask, spatial[0, 0, 0, :, low:high], both(0, 0), both(0, 1),
+            spatial[1, 0, 0, :, low:high], both(1, 0), both(1, 1),
+        )
+        for tile, pair in tiles.add(head, mask, output, output_dot):
+            for t in (0, 1):
+                attended[t * places:(t + 1) * places, tile * LANES:(tile + 1) * LANES] = pair[t].astype(jnp.bfloat16)
+        serve(head + 1)
+
+    serve_all(0)
+    all_here(0)
+    own_copies[0].wait()
+
+    @pl.loop(0, width // TILE)
+    def _(index):
+        columns = pl.ds(pl.multiple_of(index * TILE, TILE), TILE)
+        projected = across(attended[...], out_all[columns, :])
+        gate, gate_slope = mod[0:1, columns], mod[3:4, columns]
+        residual[0, 0, :, columns] = stream[0, 0, :, columns].astype(jnp.float32) + gate * projected[:places]
+        residual[1, 0, :, columns] = (
+            stream[1, 0, :, columns].astype(jnp.float32)
+            + gate_slope * projected[:places]
+            + gate * projected[places:]
+        )
+
+    serve(18)
+    row_copies = []
+    for k in list(range(1, n)) + [0]:
+        frame = lax.rem(me + k, n)
+        rows = pl.ds(pl.multiple_of(frame * part, 8), part)
+        hidden, hidden_dot = residual[0, 0, rows, :], residual[1, 0, rows, :]
+        centered = hidden - jnp.mean(hidden, axis=-1, keepdims=True)
+        inv_scale = lax.rsqrt(jnp.mean(centered * centered, axis=-1, keepdims=True) + 1e-06)
+        normed = centered * inv_scale
+        normed_dot = (
+            hidden_dot
+            - jnp.mean(hidden_dot, axis=-1, keepdims=True)
+            - normed * jnp.mean(normed * hidden_dot, axis=-1, keepdims=True)
+        ) * inv_scale
+        modulated = normed * (1.0 + mod[2:3, :]) + mod[1:2, :]
+        modulated_dot = normed_dot * (1.0 + mod[2:3, :]) + normed * mod[5:6, :] + mod[4:5, :]
+        block = jnp.concatenate([modulated, modulated_dot], axis=0).astype(jnp.bfloat16)
+        mine = pl.ds(pl.multiple_of(me * 2 * part, 16), 2 * part)
+        if k == 0:
+            rows_recv[mine, :] = block
+        else:
+            theirs = pl.ds(pl.multiple_of(frame * 2 * part, 16), 2 * part)
+            rows_send[theirs, :] = block
+            row_copies.append(remote(
+                rows_send.at[theirs], rows_recv.at[mine], row_send_sem.at[k], row_recv_sem.at[k], {"frame": frame}
+            ))
+            row_copies[-1].start()
+
+    serve_all(1)
+    all_here(1)
+    own_copies[1].wait()
+    for k in range(1, n):
+        source = lax.rem(me - k + n, n)
+        arrives(rows_recv.at[pl.ds(pl.multiple_of(source * 2 * part, 16), 2 * part)], row_recv_sem.at[k]).wait_recv()
+
+    @pl.loop(0, 3 * width // TILE)
+    def _(index):
+        columns = pl.ds(pl.multiple_of(index * TILE, TILE), TILE)
+        product = across(rows_recv[...], qkv_all[columns, :])
+        for t in (0, 1):
+            kept = [product[(2 * f + t) * part:(2 * f + t + 1) * part] for f in range(n)]
+            qkv[t, :, columns] = jnp.concatenate(kept, axis=0).astype(jnp.bfloat16)
+
+    rows = n * part
+    one = lax.rem(lax.broadcasted_iota(jnp.int32, (rows, rows), 0), part)
+    two = lax.rem(lax.broadcasted_iota(jnp.int32, (rows, rows), 1), part)
+    allowed = one == two
+    tiles = LaneTiles(heads)
+    chunks = back_send.shape[0]
+    chunk_tiles = width // LANES // chunks
+    back_copies = []
+    pieces = {}
+    for head in range(heads):
+        low, high = lane_window(head)
+        mask = head_mask(head, low, high)
+        take = lambda t, j: qkv[t, :, j * width + low:j * width + high]
+        output, output_dot = attend_head(
+            mask, take(0, 0), take(0, 1), take(0, 2), take(1, 0), take(1, 1), take(1, 2), allowed
+        )
+        for tile, pair in tiles.add(head, mask, output, output_dot):
+            chunk, inner = tile // chunk_tiles, tile % chunk_tiles
+            for f in range(n):
+                block = jnp.concatenate([value[f * part:(f + 1) * part] for value in pair], axis=0)
+                back_send[chunk, f, :, inner * LANES:(inner + 1) * LANES] = block.astype(jnp.bfloat16)
+            if inner == chunk_tiles - 1:
+                own = pltpu.make_async_copy(
+                    back_send.at[chunk, me], returned.at[chunk, me], back_send_sem.at[chunk, 0]
+                )
+                own.start()
+                back_copies.append(own)
+                for k in range(1, n):
+                    frame = lax.rem(me + k, n)
+                    copy = remote(
+                        back_send.at[chunk, frame], returned.at[chunk, me],
+                        back_send_sem.at[chunk, k], back_recv_sem.at[chunk, k], {"frame": frame},
+                    )
+                    copy.start()
+                    pieces[chunk, k] = copy
+
+    kv_copy.wait_send()
+    for which in (0, 1):
+        for step in range(1, n):
+            ring_copy(which, step).wait_send()
+            core_copy(which, step).wait_send()
+
+            @pl.when(core == 0)
+            def _():
+                x_copy(which, step).wait_send()
+                xcore_copy(which, step).wait_send()
+
+    for copy in row_copies:
+        copy.wait_send()
+    for copy in back_copies:
+        copy.wait()
+    for (chunk, k), copy in pieces.items():
+        copy.wait_send()
+        source = lax.rem(me - k + n, n)
+        arrives(returned.at[chunk, source], back_recv_sem.at[chunk, k]).wait_recv()
+
+
+def per_device_fused(n, stream, spatial_qkv, out_weight, qkv_weight, mod_table, timestep):
+    places, width = stream.shape[2], stream.shape[3]
+    part = places // n
+    chunks = width // TILE
+    mod = jnp.concatenate(modulation(mod_table, timestep), axis=0)
+    bf16, f32 = jnp.bfloat16, jnp.float32
+    dma = pltpu.SemaphoreType.DMA
+    vmem = pl.BlockSpec(memory_space=pltpu.VMEM)
+    residual, returned = pl.pallas_call(
+        functools.partial(fused_kernel, n),
+        out_shape=(
+            jax.ShapeDtypeStruct(stream.shape, f32),
+            jax.ShapeDtypeStruct((chunks, n, 2 * part, TILE), bf16),
+        ),
+        in_specs=[vmem] * 5,
+        out_specs=(vmem, vmem),
+        scratch_shapes=[
+            pltpu.VMEM((2, 2, places, width), bf16),
+            pltpu.VMEM((width, width), bf16),
+            pltpu.VMEM((3 * width, width), bf16),
+            pltpu.VMEM((2 * places, width), bf16),
+            pltpu.VMEM((2 * places, width), bf16),
+            pltpu.VMEM((2 * places, width), bf16),
+            pltpu.VMEM((2, places, 3 * width), bf16),
+            pltpu.VMEM((chunks, n, 2 * part, TILE), bf16),
+            dma((2,)), dma((2,)),
+        ] + [dma((2, n))] * 8 + [dma((n,))] * 2 + [dma((chunks, n))] * 2,
+        compiler_params=pltpu.CompilerParams(
+            collective_id=0, has_side_effects=True, vmem_limit_bytes=56 * 1024 * 1024
+        ),
+    )(spatial_qkv, stream, out_weight.T, qkv_weight.T, mod)
+    temporal = returned.reshape(chunks, n, 2, part, TILE)
+    temporal = jnp.transpose(temporal, (2, 1, 3, 0, 4)).reshape(stream.shape).astype(f32)
+    return (residual, temporal)
+
+
+def fits_fused(mesh, places, width, out_columns, qkv_columns, frames_local):
+    n = mesh.shape["frame"]
+    return (
+        mesh.shape["pix"] == 2
+        and mesh.shape["clips"] % 2 == 0
+        and n % 2 == 0
+        and frames_local == 1
+        and places % n == 0
+        and (places // n) % 8 == 0
+        and places % 16 == 0
+        and width % TILE == 0
+        and width % HEAD_DIM == 0
+        and out_columns % 48 == 0
+        and qkv_columns % 48 == 0
+    )
+
+
 def solution(mesh):
     in_specs = (
         P(None, ("clips", "frame"), "pix", None),
@@ -128,6 +509,13 @@
         P("clips"),
     )
     out_specs = (P(None, ("clips", "frame"), "pix", None), P(None, ("clips", "frame"), "pix", None))
-    return jax.shard_map(
-        per_device, mesh=mesh, in_specs=in_specs, out_specs=out_specs, check_vma=False
-    )
+
+    def local(stream, spatial_qkv, out_weight, qkv_weight, mod_table, timestep):
+        args = (stream, spatial_qkv, out_weight, qkv_weight, mod_table, timestep)
+        if fits_fused(
+            mesh, stream.shape[2], stream.shape[3], out_weight.shape[1], qkv_weight.shape[1], stream.shape[1]
+        ):
+            return per_device_fused(mesh.shape["frame"], *args)
+        return per_device(*args)
+
+    return jax.shard_map(local, mesh=mesh, in_specs=in_specs, out_specs=out_specs, check_vma=False)

time: 313 us -> 126 us (0.40)
  waiting for transfers between devices: 134 us -> 0 us
  Pallas kernels: 0 us -> 115 us
  blocking collectives: 52.7 us -> 0 us
  local copies, waits for them, and re-layouts: 55.6 us -> 7.85 us
  matrix products: 38.4 us -> 0 us
  between operations: 15 us -> 1.31 us
  starting transfers between devices: 9.5 us -> 0 us
  other arithmetic: 5.64 us -> 0.71 us
    pallas_call x0 -> x1, Pallas kernels: none -> 115 us  [per_device_fused(): pl.pallas_call(functools.partial(fused_kernel, n), out_shape=(jax.ShapeDt...]
    all_gather x2 -> x0, waiting for transfers between devices: 89 us -> none  [the longest x1 84 us: per_device(): lax.all_gather(qkv_weight, 'frame', axis=1, tiled=True)]
    all_to_all x2 -> x0, blocking collectives: 52.7 us -> none  [the longest x1 48.1 us: per_device(): lax.all_to_all(modulated_low, 'frame', split_axis=2, concat_axis=1, tiled...]
    all_to_all x2 -> x0, waiting for transfers between devices: 43.8 us -> none  [the longest x1 39.7 us: per_device(): lax.all_to_all(attended, 'frame', split_axis=1, concat_axis=2, tiled=True)]
    dot_general x55 -> x0, matrix products: 34 us -> none  [the longest x1 9.33 us: per_device(): jnp.dot(flat_rows, lax.all_gather(qkv_weight, 'frame', axis=1, tiled=True...]
    another operation x6 -> x0, local copies, waits for them, and re-layouts: 20.1 us -> none  [the longest x1 12.7 us: attend(): shaped = jnp.transpose(shaped, (4, 0, 1, 2, 3, 5, 6))]
    all_to_all x2 -> x0, starting transfers between devices: 9.42 us -> none  [the longest x1 5.83 us: per_device(): lax.all_to_all(spatial_qkv, 'pix', split_axis=4, concat_axis=3, tiled=True)]
    all_to_all x5 -> x0, local copies, waits for them, and re-layouts: 9.15 us -> none  [the longest x1 6.61 us: per_device(): lax.all_to_all(spatial_qkv, 'pix', split_axis=4, concat_axis=3, tiled=True)]
  transfers between devices with their start and end apart: 4 -> 0, of which waited for: 4 -> 0; matrix products, arithmetic and copies ran while one was open for 15% -> 0% of each run, Pallas kernels for 0% -> 0%
where the time goes in v1:
time: 126 us; the launch traced here: 125 us
  Pallas kernels  115 us (91%)
  local copies, waits for them, and re-layouts  7.85 us (6%)
  between operations  1.31 us (1%)
    pallas_call x1, Pallas kernels, per_device_fused(): pl.pallas_call(functools.partial(fused_kernel, n), out_shape=(jax.ShapeDt...  115 us
    convert_element_type x2, local copies, waits for them, and re-layouts, per_device_fused(): jnp.transpose(temporal, (2, 1, 3, 0, 4)).reshape(stream.shape).astype(f32)  4.2 us
    unnamed x1, local copies, waits for them, and re-layouts  2.8 us

profile of v1, /device:TPU:0, one launch (start us, length us, event | category | flops | bytes accessed | tf_op | source)
XLA Modules:
  0.0 125.1 jit_solution(15130382122937743476)
XLA Ops:
  1.3 0.1 multiply_sine_fusion
  1.4 0.8 fusion.5
  2.2 0.6 pad_maximum_fusion.mod
  2.9 115.2 %shard_map.77 = (f32[2,1,192,1152]{3,2,1,0:T(8,128)}, bf16[3,8,48,384]{3,2,1,0:T(8,128)(2,1)}) custom-call(bf16[2,3,1,192,1152]{4,3,2,1,0:T(8,128)(2,1)} %spatial.1, bf16[2,1,192,1152]{3,2,1,0:T(8,128)(2,1)} %stream.1, bf16[144,1152]{1,0:T(8,128)(2,1)} %bitcast.29, bf16[432,1152]{1,0:T(8,128)(2,1)} %bitcast.27, f32[6,1152]{1,0:T(8,128)} %pad_maximum_fusion.mod), custom_call_target="tpu_custom_call" | custom-call | tf_op jit(solution)/shard_map/pallas_call | solution.py:457
  118.1 1.9 %copy.32 = f32[3,8,2,24,384]{4,0,3,1,2:T(4,128)S(1)} copy(bf16[3,8,2,24,384]{4,3,2,1,0:T(8,128)(2,1)} %bitcast.28) | data formatting | bytes 2654208 | tf_op jit(solution)/shard_map/convert_element_type | solution.py:481
  120.0 2.3 %reshape.38 = f32[2,1,192,1152]{3,2,0,1:T(8,128)} reshape(f32[2,8,24,3,384]{4,3,2,1,0:T(4,128)S(1)} %bitcast.25) | data formatting | bytes 3538944 | tf_op jit(solution)/shard_map/convert_element_type | solution.py:481
  122.3 2.8 %copy.35 = f32[2,1,192,1152]{3,2,1,0:T(8,128)} copy(f32[2,1,192,1152]{3,2,1,0:T(8,128)} %get-tuple-element.16) | data formatting | bytes 3538944
  (2 shorter events, 0.0 us)

commit v2 on v1

--- a/solution.py
+++ b/solution.py
@@ -186,7 +186,7 @@
 def fused_kernel(
     n, spatial, stream, out_own, qkv_own, mod, residual, returned,
     peer_kv, out_all, qkv_all, attended, rows_send, rows_recv, qkv, back_send,
-    kv_sem, own_sem, ring_send, ring_recv, core_send, core_recv, x_send, x_recv,
+    kv_sem, own_sem, up_send, down_send, row_send, grid_recv, core_send, core_recv, x_send, x_recv,
     xcore_send, xcore_recv, row_send_sem, row_recv_sem, back_send_sem, back_recv_sem,
 ):
     clip, core, me = lax.axis_index("clips"), lax.axis_index("pix"), lax.axis_index("frame")
@@ -197,21 +197,11 @@
     heads = width // HEAD_DIM
     half = n // 2
 
-    depth_of = lambda frame: lax.div(frame, 2)
-    row_of = lambda frame: lax.rem(frame, 2)
-    place_of = lambda frame: depth_of(frame) * (1 - row_of(frame)) + (n - 1 - depth_of(frame)) * row_of(frame)
-
-    def frame_at(place):
-        later = lax.div(place, half)
-        return (1 - later) * (2 * place) + later * (2 * (n - 1 - place) + 1)
-
-    place = place_of(me)
-    step_by = 1 - 2 * core
-    behind = lambda steps: frame_at(lax.rem(place - steps * step_by + 2 * n, n))
-    after = behind(-1)
+    depth, row = lax.div(me, 2), lax.rem(me, 2)
+    depths = n // 2
     to_peer = {"pix": 1 - core}
     to_x = {"clips": x_peer}
-    to_next = {"frame": after}
+    to_row = {"frame": 2 * depth + 1 - row}
 
     barrier = pltpu.get_barrier_semaphore()
     for target in [to_peer, to_x] + [{"frame": lax.rem(me + k, n)} for k in range(1, n)]:
@@ -238,82 +228,137 @@
         size = sizes[which] // 3
         return gathered[which].at[pl.ds(pl.multiple_of(frame * sizes[which] + third * size, 16), size)]
 
-    def ring_copy(which, step):
-        block = piece(which, behind(step - 1), my_third)
-        if step == 1:
-            size = sizes[which] // 3
-            source = owned[which].at[pl.ds(pl.multiple_of(my_third * size, 16), size)]
-        else:
-            source = block
-        return remote(source, block, ring_send.at[which, step], ring_recv.at[which, step], to_next)
-
     def arrives(block, recv):
         return remote(block, block, kv_sem.at[0], recv, to_peer)
 
-    def core_copy(which, step):
-        block = piece(which, behind(step), my_third)
-        return remote(block, block, core_send.at[which, step], core_recv.at[which, step], to_peer)
-
-    def x_copy(which, step):
-        block = piece(which, behind(step), my_third)
-        return remote(block, block, x_send.at[which, step], x_recv.at[which, step], to_x)
-
-    def xcore_copy(which, step):
-        block = piece(which, behind(step), x_third)
-        return remote(block, block, xcore_send.at[which, step], xcore_recv.at[which, step], to_peer)
-
-    def ring_step(which, step):
-        arrives(piece(which, behind(step), my_third), ring_recv.at[which, step]).wait_recv()
-        if step < n - 1:
-            ring_copy(which, step + 1).start()
-
-        @pl.when(core == 0)
-        def _():
-            x_copy(which, step).start()
-
-        core_copy(which, step).start()
-
-    def x_step(which, step):
-        @pl.when(core == 0)
-        def _():
-            arrives(piece(which, behind(step), x_third), x_recv.at[which, step]).wait_recv()
-            xcore_copy(which, step).start()
+    def moves(which, frame, third, send, recv, device):
+        block = piece(which, frame, third)
+        return remote(block, block, send.at[which, frame], recv.at[which, frame], device)
+
+    def own_move(which, send, device):
+        size = sizes[which] // 3
+        source = owned[which].at[pl.ds(pl.multiple_of(my_third * size, 16), size)]
+        return remote(
+            source, piece(which, me, my_third), send.at[which, me], grid_recv.at[which, me], device
+        )
+
+    line_copy = lambda which, frame, sign: moves(
+        which, frame, my_third, up_send if sign > 0 else down_send, grid_recv, {"frame": me + 2 * sign}
+    )
+    row_copy = lambda which, frame: moves(which, frame, my_third, row_send, grid_recv, to_row)
+    core_copy = lambda which, frame: moves(which, frame, my_third, core_send, core_recv, to_peer)
+    x_copy = lambda which, frame: moves(which, frame, my_third, x_send, x_recv, to_x)
+    xcore_copy = lambda which, frame: moves(which, frame, x_third, xcore_send, xcore_recv, to_peer)
+
+    def inside(offset):
+        return (depth + offset >= 0) & (depth + offset < depths)
+
+    def when_core(which_core, act):
+        pl.when(core == which_core)(act)
+
+    def line_step(which, distance):
+        for sign in (1, -1):
+            @pl.when(inside(-sign * distance))
+            def _():
+                frame = me - 2 * sign * distance
+                arrives(piece(which, frame, my_third), grid_recv.at[which, frame]).wait_recv()
+
+                @pl.when(inside(sign))
+                def _():
+                    line_copy(which, frame, sign).start()
+
+                row_copy(which, frame).start()
+                when_core(0, lambda: x_copy(which, frame).start())
+                core_copy(which, frame).start()
+
+    def offsets(distance):
+        return (1, -1) if distance else (1,)
+
+    def row_step(which, distance):
+        for sign in offsets(distance):
+            @pl.when(inside(sign * distance))
+            def _():
+                frame = 2 * (depth + sign * distance) + 1 - row
+                arrives(piece(which, frame, my_third), grid_recv.at[which, frame]).wait_recv()
+                when_core(0, lambda: x_copy(which, frame).start())
+                core_copy(which, frame).start()
+
+    def x_step(which, distance, turn):
+        for sign in offsets(distance):
+            @pl.when(inside(sign * distance) & (core == 0))
+            def _():
+                frame = 2 * (depth + sign * distance) + (1 - turn) * row + turn * (1 - row)
+                arrives(piece(which, frame, x_third), x_recv.at[which, frame]).wait_recv()
+                xcore_copy(which, frame).start()
 
     def all_here(which):
-        for step in range(1, n):
-            other = frame_at(lax.rem(place + step * step_by + 2 * n, n))
-            arrives(piece(which, other, peer_third), core_recv.at[which, step]).wait_recv()
-
-        @pl.when(core == 1)
-        def _():
-            for step in range(1, n):
-                other = frame_at(lax.rem(place + step * step_by + 2 * n, n))
-                arrives(piece(which, other, x_third), xcore_recv.at[which, step]).wait_recv()
+        for k in range(1, n):
+            frame = lax.rem(me + k, n)
+            arrives(piece(which, frame, peer_third), core_recv.at[which, frame]).wait_recv()
+            when_core(
+                1, lambda: arrives(piece(which, frame, x_third), xcore_recv.at[which, frame]).wait_recv()
+            )
+
+    def all_sent(which):
+        own_move(which, row_send, to_row).wait_send()
+        for sign in (1, -1):
+            @pl.when(inside(sign))
+            def _():
+                own_move(which, up_send if sign > 0 else down_send, {"frame": me + 2 * sign}).wait_send()
+
+            for distance in range(1, depths):
+                @pl.when(inside(-sign * distance))
+                def _():
+                    frame = me - 2 * sign * distance
+                    row_copy(which, frame).wait_send()
+
+                    @pl.when(inside(sign))
+                    def _():
+                        line_copy(which, frame, sign).wait_send()
+
+        for k in range(1, n):
+            frame = lax.rem(me + k, n)
+            core_copy(which, frame).wait_send()
+
+            @pl.when(core == 0)
+            def _():
+                x_copy(which, frame).wait_send()
+                xcore_copy(which, frame).wait_send()
 
     own_copies = []
     for which in (0, 1):
-        ring_copy(which, 1).start()
+        for sign in (1, -1):
+            @pl.when(inside(sign))
+            def _():
+                own_move(which, up_send if sign > 0 else down_send, {"frame": me + 2 * sign}).start()
+
+        own_move(which, row_send, to_row).start()
         whole = gathered[which].at[pl.ds(pl.multiple_of(me * sizes[which], 16), sizes[which])]
         own_copies.append(pltpu.make_async_copy(owned[which], whole, own_sem.at[which]))
         own_copies[-1].start()
 
     events = []
-    for step in range(1, n):
-        events.append((2.0 * step, ring_step, 0, step))
-        events.append((2.0 * step + 2.0, x_step, 0, step))
-        events.append((4.0 * step, ring_step, 1, step))
-        events.append((4.0 * step + 3.0, x_step, 1, step))
+    for distance in range(depths):
+        if distance:
+            events.append((2 * distance, line_step, (0, distance)))
+            events.append((4 * distance + 1, line_step, (1, distance)))
+            events.append((2 * distance + 3, x_step, (0, distance, 0)))
+            events.append((4 * distance + 6, x_step, (1, distance, 0)))
+        events.append((2 * distance + 2.5, row_step, (0, distance)))
+        events.append((4 * distance + 5, row_step, (1, distance)))
+        events.append((2 * distance + 5, x_step, (0, distance, 1)))
+        events.append((4 * distance + 8, x_step, (1, distance, 1)))
     events.sort(key=lambda event: event[0])
 
     def serve(until):
         while events and events[0][0] <= until:
-            _, act, which, step = events.pop(0)
-            act(which, step)
+            _, act, args = events.pop(0)
+            act(*args)
 
     def serve_all(which):
-        for event in [event for event in events if event[2] == which]:
+        for event in [event for event in events if event[2][0] == which]:
             events.remove(event)
-            event[1](event[2], event[3])
+            event[1](*event[2])
 
     kv_copy.wait_recv()
     tiles = LaneTiles(heads)
@@ -346,7 +391,7 @@
             + gate * projected[places:]
         )
 
-    serve(18)
+    serve(17)
     row_copies = []
     for k in list(range(1, n)) + [0]:
         frame = lax.rem(me + k, n)
@@ -373,6 +418,7 @@
                 rows_send.at[theirs], rows_recv.at[mine], row_send_sem.at[k], row_recv_sem.at[k], {"frame": frame}
             ))
             row_copies[-1].start()
+        serve(18 + k)
 
     serve_all(1)
     all_here(1)
@@ -381,13 +427,14 @@
         source = lax.rem(me - k + n, n)
         arrives(rows_recv.at[pl.ds(pl.multiple_of(source * 2 * part, 16), 2 * part)], row_recv_sem.at[k]).wait_recv()
 
-    @pl.loop(0, 3 * width // TILE)
-    def _(index):
-        columns = pl.ds(pl.multiple_of(index * TILE, TILE), TILE)
-        product = across(rows_recv[...], qkv_all[columns, :])
-        for t in (0, 1):
-            kept = [product[(2 * f + t) * part:(2 * f + t + 1) * part] for f in range(n)]
-            qkv[t, :, columns] = jnp.concatenate(kept, axis=0).astype(jnp.bfloat16)
+    def project_chunk(chunk):
+        @pl.loop(0, 3)
+        def _(index):
+            columns = pl.ds(pl.multiple_of(index * width + chunk * TILE, LANES), TILE)
+            product = across(rows_recv[...], qkv_all[columns, :])
+            for t in (0, 1):
+                kept = [product[(2 * f + t) * part:(2 * f + t + 1) * part] for f in range(n)]
+                qkv[t, :, columns] = jnp.concatenate(kept, axis=0).astype(jnp.bfloat16)
 
     rows = n * part
     one = lax.rem(lax.broadcasted_iota(jnp.int32, (rows, rows), 0), part)
@@ -398,8 +445,12 @@
     chunk_tiles = width // LANES // chunks
     back_copies = []
     pieces = {}
+    ready = 0
     for head in range(heads):
         low, high = lane_window(head)
+        while ready * TILE < high:
+            project_chunk(ready)
+            ready += 1
         mask = head_mask(head, low, high)
         take = lambda t, j: qkv[t, :, j * width + low:j * width + high]
         output, output_dot = attend_head(
@@ -427,15 +478,7 @@
 
     kv_copy.wait_send()
     for which in (0, 1):
-        for step in range(1, n):
-            ring_copy(which, step).wait_send()
-            core_copy(which, step).wait_send()
-
-            @pl.when(core == 0)
-            def _():
-                x_copy(which, step).wait_send()
-                xcore_copy(which, step).wait_send()
-
+        all_sent(which)
     for copy in row_copies:
         copy.wait_send()
     for copy in back_copies:
@@ -444,6 +487,21 @@
         copy.wait_send()
         source = lax.rem(me - k + n, n)
         arrives(returned.at[chunk, source], back_recv_sem.at[chunk, k]).wait_recv()
+
+
+def finish_kernel(residual, returned, residual_out, temporal, sem):
+    copy = pltpu.make_async_copy(residual, residual_out, sem)
+    copy.start()
+    chunks, n, rows, tile = returned.shape
+    part = rows // 2
+    for chunk in range(chunks):
+        for f in range(n):
+            block = returned[chunk, f].astype(jnp.float32)
+            for t in (0, 1):
+                temporal[t, 0, f * part:(f + 1) * part, chunk * tile:(chunk + 1) * tile] = (
+                    block[t * part:(t + 1) * part]
+                )
+    copy.wait()
 
 
 def per_device_fused(n, stream, spatial_qkv, out_weight, qkv_weight, mod_table, timestep):
@@ -472,14 +530,19 @@
             pltpu.VMEM((2, places, 3 * width), bf16),
             pltpu.VMEM((chunks, n, 2 * part, TILE), bf16),
             dma((2,)), dma((2,)),
-        ] + [dma((2, n))] * 8 + [dma((n,))] * 2 + [dma((chunks, n))] * 2,
+        ] + [dma((2, n))] * 10 + [dma((n,))] * 2 + [dma((chunks, n))] * 2,
         compiler_params=pltpu.CompilerParams(
             collective_id=0, has_side_effects=True, vmem_limit_bytes=56 * 1024 * 1024
         ),
     )(spatial_qkv, stream, out_weight.T, qkv_weight.T, mod)
-    temporal = returned.reshape(chunks, n, 2, part, TILE)
-    temporal = jnp.transpose(temporal, (2, 1, 3, 0, 4)).reshape(stream.shape).astype(f32)
-    return (residual, temporal)
+    return tuple(pl.pallas_call(
+        finish_kernel,
+        out_shape=(jax.ShapeDtypeStruct(stream.shape, f32),) * 2,
+        in_specs=[pl.BlockSpec(memory_space=pl.ANY), vmem],
+        out_specs=(pl.BlockSpec(memory_space=pl.ANY), vmem),
+        scratch_shapes=[dma],
+        compiler_params=pltpu.CompilerParams(vmem_limit_bytes=32 * 1024 * 1024),
+    )(residual, returned))
 
 
 def fits_fused(mesh, places, width, out_columns, qkv_columns, frames_local):

time: 126 us -> 107 us (0.85)
  Pallas kernels: 115 us -> 101 us
  local copies, waits for them, and re-layouts: 7.85 us -> 3.48 us
    pallas_call x1, Pallas kernels: 115 us -> 99 us  [per_device_fused(): pl.pallas_call(functools.partial(fused_kernel, n), out_shape=(jax.ShapeDt...]
    convert_element_type x2 -> x0, local copies, waits for them, and re-layouts: 4.2 us -> none  [per_device_fused(): jnp.transpose(temporal, (2, 1, 3, 0, 4)).reshape(stream.shape).astype(f32)]
    pallas_call x0 -> x1, Pallas kernels: none -> 2.42 us  [per_device_fused(): pl.pallas_call(finish_kernel, out_shape=(jax.ShapeDtypeStruct(stream.shap...]
    unnamed x1 -> x4, local copies, waits for them, and re-layouts: 2.8 us -> 2.64 us
where the time goes in v2:
time: 107 us
  Pallas kernels  101 us (94%)
  local copies, waits for them, and re-layouts  3.48 us (3%)
  between operations  1.48 us (1%)
    pallas_call x1, Pallas kernels, per_device_fused(): pl.pallas_call(functools.partial(fused_kernel, n), out_shape=(jax.ShapeDt...  99 us
    unnamed x4, local copies, waits for them, and re-layouts  2.64 us
    pallas_call x1, Pallas kernels, per_device_fused(): pl.pallas_call(finish_kernel, out_shape=(jax.ShapeDtypeStruct(stream.shap...  2.42 us

profile of v2, /device:TPU:0, one launch (start us, length us, event | category | flops | bytes accessed | tf_op | source)
XLA Modules:
  0.0 107.1 jit_solution(9605895434839027587)
XLA Ops:
  1.3 0.1 multiply_sine_fusion
  1.4 0.8 fusion.5
  2.2 0.6 pad_maximum_fusion.mod
  2.9 99.0 %shard_map.77 = (f32[2,1,192,1152]{3,2,1,0:T(8,128)}, bf16[3,8,48,384]{3,2,1,0:T(8,128)(2,1)}) custom-call(bf16[2,3,1,192,1152]{4,3,2,1,0:T(8,128)(2,1)} %spatial.1, bf16[2,1,192,1152]{3,2,1,0:T(8,128)(2,1)} %stream.1, bf16[144,1152]{1,0:T(8,128)(2,1)} %bitcast.20, bf16[432,1152]{1,0:T(8,128)(2,1)} %bitcast.19, f32[6,1152]{1,0:T(8,128)} %pad_maximum_fusion.mod), custom_call_target="tpu_custom_call" | custom-call | tf_op jit(solution)/shard_map/pallas_call | solution.py:515
  101.9 0.0 copy-start
  101.9 1.5 %copy-done = f32[2,1,192,1152]{3,2,1,0:T(8,128)S(1)} copy-done((f32[2,1,192,1152]{3,2,1,0:T(8,128)S(1)}, f32[2,1,192,1152]{3,2,1,0:T(8,128)}, u32[]{:S(2)}) %copy-start) | copy-done | bytes 1769496
  103.4 0.0 copy-start.1
  103.4 1.2 %copy-done.1 = bf16[3,8,48,384]{3,2,1,0:T(8,128)(2,1)S(1)} copy-done((bf16[3,8,48,384]{3,2,1,0:T(8,128)(2,1)S(1)}, bf16[3,8,48,384]{3,2,1,0:T(8,128)(2,1)}, u32[]{:S(2)}) %copy-start.1) | copy-done | bytes 884760
  104.5 2.4 %shard_map.78 = (f32[2,1,192,1152]{3,2,1,0:T(8,128)}, f32[2,1,192,1152]{3,2,1,0:T(8,128)}) custom-call(f32[2,1,192,1152]{3,2,1,0:T(8,128)S(1)} %copy-done, bf16[3,8,48,384]{3,2,1,0:T(8,128)(2,1)S(1)} %copy-done.1), custom_call_target="tpu_custom_call" | custom-call | tf_op jit(solution)/shard_map/pallas_call | solution.py:538
  (2 shorter events, 0.0 us)
Async XLA Ops:
  101.9 1.5 %copy-start = (f32[2,1,192,1152]{3,2,1,0:T(8,128)S(1)}, f32[2,1,192,1152]{3,2,1,0:T(8,128)}, u32[]{:S(2)}) copy-start(f32[2,1,192,1152]{3,2,1,0:T(8,128)} %get-tuple-element.4.residual) | copy-start | bytes 5308420
  103.4 1.2 %copy-start.1 = (bf16[3,8,48,384]{3,2,1,0:T(8,128)(2,1)S(1)}, bf16[3,8,48,384]{3,2,1,0:T(8,128)(2,1)}, u32[]{:S(2)}) copy-start(bf16[3,8,48,384]{3,2,1,0:T(8,128)(2,1)} %get-tuple-element.5.returned) | copy-start | bytes 2654212

commit v3 on v2

--- a/solution.py
+++ b/solution.py
@@ -341,13 +341,13 @@
     for distance in range(depths):
         if distance:
             events.append((2 * distance, line_step, (0, distance)))
-            events.append((4 * distance + 1, line_step, (1, distance)))
+            events.append((14 + 4 * (distance - 1), line_step, (1, distance)))
             events.append((2 * distance + 3, x_step, (0, distance, 0)))
-            events.append((4 * distance + 6, x_step, (1, distance, 0)))
+            events.append((16 + 5 * (distance - 1), x_step, (1, distance, 0)))
         events.append((2 * distance + 2.5, row_step, (0, distance)))
-        events.append((4 * distance + 5, row_step, (1, distance)))
+        events.append((14.5 + 4.5 * distance, row_step, (1, distance)))
         events.append((2 * distance + 5, x_step, (0, distance, 1)))
-        events.append((4 * distance + 8, x_step, (1, distance, 1)))
+        events.append((16.5 + 5 * distance, x_step, (1, distance, 1)))
     events.sort(key=lambda event: event[0])
 
     def serve(until):
@@ -418,7 +418,6 @@
                 rows_send.at[theirs], rows_recv.at[mine], row_send_sem.at[k], row_recv_sem.at[k], {"frame": frame}
             ))
             row_copies[-1].start()
-        serve(18 + k)
 
     serve_all(1)
     all_here(1)
@@ -489,19 +488,28 @@
         arrives(returned.at[chunk, source], back_recv_sem.at[chunk, k]).wait_recv()
 
 
-def finish_kernel(residual, returned, residual_out, temporal, sem):
-    copy = pltpu.make_async_copy(residual, residual_out, sem)
-    copy.start()
+def finish_kernel(residual, returned, residual_out, temporal_out, blocks, temporal, sem):
     chunks, n, rows, tile = returned.shape
     part = rows // 2
+    arrivals = [pltpu.make_async_copy(returned.at[c], blocks.at[c], sem.at[c]) for c in range(chunks)]
+    leaving = [pltpu.make_async_copy(residual.at[t], residual_out.at[t], sem.at[2 * chunks + t]) for t in (0, 1)]
+    for copy in arrivals + leaving:
+        copy.start()
     for chunk in range(chunks):
+        arrivals[chunk].wait()
         for f in range(n):
-            block = returned[chunk, f].astype(jnp.float32)
+            block = blocks[chunk, f].astype(jnp.float32)
             for t in (0, 1):
                 temporal[t, 0, f * part:(f + 1) * part, chunk * tile:(chunk + 1) * tile] = (
                     block[t * part:(t + 1) * part]
                 )
-    copy.wait()
+        columns = pl.ds(chunk * tile, tile)
+        leaving.append(pltpu.make_async_copy(
+            temporal.at[:, :, :, columns], temporal_out.at[:, :, :, columns], sem.at[chunks + chunk]
+        ))
+        leaving[-1].start()
+    for copy in leaving:
+        copy.wait()
 
 
 def per_device_fused(n, stream, spatial_qkv, out_weight, qkv_weight, mod_table, timestep):
@@ -538,10 +546,12 @@
     return tuple(pl.pallas_call(
         finish_kernel,
         out_shape=(jax.ShapeDtypeStruct(stream.shape, f32),) * 2,
-        in_specs=[pl.BlockSpec(memory_space=pl.ANY), vmem],
-        out_specs=(pl.BlockSpec(memory_space=pl.ANY), vmem),
-        scratch_shapes=[dma],
-        compiler_params=pltpu.CompilerParams(vmem_limit_bytes=32 * 1024 * 1024),
+        in_specs=[pl.BlockSpec(memory_space=pl.ANY)] * 2,
+        out_specs=(pl.BlockSpec(memory_space=pl.ANY),) * 2,
+        scratch_shapes=[
+            pltpu.VMEM((chunks, n, 2 * part, TILE), bf16), pltpu.VMEM(stream.shape, f32), dma((2 * chunks + 2,))
+        ],
+        compiler_params=pltpu.CompilerParams(vmem_limit_bytes=56 * 1024 * 1024),
     )(residual, returned))
 
 

time: 107 us -> 161 us (1.50)
  Pallas kernels: 101 us -> 157 us
  local copies, waits for them, and re-layouts: 3.48 us -> 0.85 us
    pallas_call x1, Pallas kernels: 2.42 us -> 54.8 us  [per_device_fused(): pl.pallas_call(finish_kernel, out_shape=(jax.ShapeDtypeStruct(stream.shap...]
    pallas_call x1, Pallas kernels: 99 us -> 102 us  [per_device_fused(): pl.pallas_call(functools.partial(fused_kernel, n), out_shape=(jax.ShapeDt...]
    unnamed x4 -> x0, local copies, waits for them, and re-layouts: 2.64 us -> none
where the time goes in v3:
time: 161 us; the launch traced here: 160 us
  Pallas kernels  157 us (98%)
    pallas_call x1, Pallas kernels, per_device_fused(): pl.pallas_call(functools.partial(fused_kernel, n), out_shape=(jax.ShapeDt...  102 us
    pallas_call x1, Pallas kernels, per_device_fused(): pl.pallas_call(finish_kernel, out_shape=(jax.ShapeDtypeStruct(stream.shap...  54.8 us

profile of v3, /device:TPU:0, one launch (start us, length us, event | category | flops | bytes accessed | tf_op | source)
XLA Modules:
  0.0 159.7 jit_solution(16359287083792442634)
XLA Ops:
  1.3 0.1 multiply_sine_fusion
  1.4 0.8 fusion.5
  2.2 0.6 pad_maximum_fusion.mod
  2.9 101.9 %shard_map.77 = (f32[2,1,192,1152]{3,2,1,0:T(8,128)}, bf16[3,8,48,384]{3,2,1,0:T(8,128)(2,1)}) custom-call(bf16[2,3,1,192,1152]{4,3,2,1,0:T(8,128)(2,1)} %spatial.1, bf16[2,1,192,1152]{3,2,1,0:T(8,128)(2,1)} %stream.1, bf16[144,1152]{1,0:T(8,128)(2,1)} %bitcast.20, bf16[432,1152]{1,0:T(8,128)(2,1)} %bitcast.19, f32[6,1152]{1,0:T(8,128)} %pad_maximum_fusion.mod), custom_call_target="tpu_custom_call" | custom-call | tf_op jit(solution)/shard_map/pallas_call | solution.py:523
  104.7 54.8 %shard_map.78 = (f32[2,1,192,1152]{3,2,1,0:T(8,128)}, f32[2,1,192,1152]{3,2,1,0:T(8,128)}) custom-call(f32[2,1,192,1152]{3,2,1,0:T(8,128)} %get-tuple-element.4.residual, bf16[3,8,48,384]{3,2,1,0:T(8,128)(2,1)} %get-tuple-element.5.returned), custom_call_target="tpu_custom_call" | custom-call | tf_op jit(solution)/shard_map/pallas_call | solution.py:546
  (2 shorter events, 0.0 us)

commit v4 on v3

--- a/solution.py
+++ b/solution.py
@@ -145,18 +145,18 @@
     query = query * keep
     query_dot = query_dot * keep
     both = across(jnp.concatenate([query, query_dot], axis=0), keys)
-    scores = both[:rows] * scale
-    scores_dot = (both[rows:] + across(query, keys_dot)) * scale
+    scores = both[:rows]
+    scores_dot = both[rows:] + across(query, keys_dot)
     if allowed is not None:
         scores = jnp.where(allowed, scores, -jnp.inf)
-    expo = jnp.exp(scores - jnp.max(scores, axis=-1, keepdims=True))
-    probs = expo * (1.0 / jnp.sum(expo, axis=-1, keepdims=True))
-    weighted = probs * (scores_dot - jnp.sum(probs * scores_dot, axis=-1, keepdims=True))
-    probs_low = probs.astype(jnp.bfloat16)
-    stacked = jnp.concatenate([probs_low, weighted.astype(jnp.bfloat16)], axis=0)
+    expo = jnp.exp((scores - jnp.max(scores, axis=-1, keepdims=True)) * scale)
+    inverse = 1.0 / jnp.sum(expo, axis=-1, keepdims=True)
+    weighted = expo * (scores_dot - inverse * jnp.sum(expo * scores_dot, axis=-1, keepdims=True))
+    expo_low = expo.astype(jnp.bfloat16)
+    stacked = jnp.concatenate([expo_low, weighted.astype(jnp.bfloat16)], axis=0)
     both = jnp.dot(stacked, values, preferred_element_type=jnp.float32)
-    output_dot = both[rows:] + jnp.dot(probs_low, values_dot, preferred_element_type=jnp.float32)
-    return both[:rows], output_dot
+    output_dot = both[rows:] * scale + jnp.dot(expo_low, values_dot, preferred_element_type=jnp.float32)
+    return both[:rows] * inverse, output_dot * inverse
 
 
 class LaneTiles:
@@ -184,8 +184,8 @@
 
 
 def fused_kernel(
-    n, spatial, stream, out_own, qkv_own, mod, residual, returned,
-    peer_kv, out_all, qkv_all, attended, rows_send, rows_recv, qkv, back_send,
+    n, spatial_in, stream_in, out_own, qkv_own, mod, residual_out, returned,
+    spatial, stream, residual, in_sem, peer_kv, out_all, qkv_all, attended, rows_send, rows_recv, qkv, back_send,
     kv_sem, own_sem, up_send, down_send, row_send, grid_recv, core_send, core_recv, x_send, x_recv,
     xcore_send, xcore_recv, row_send_sem, row_recv_sem, back_send_sem, back_recv_sem,
 ):
@@ -203,6 +203,10 @@
     to_x = {"clips": x_peer}
     to_row = {"frame": 2 * depth + 1 - row}
 
+    spatial_copy = pltpu.make_async_copy(spatial_in, spatial, in_sem.at[0])
+    stream_copy = pltpu.make_async_copy(stream_in, stream, in_sem.at[1])
+    spatial_copy.start()
+
     barrier = pltpu.get_barrier_semaphore()
     for target in [to_peer, to_x] + [{"frame": lax.rem(me + k, n)} for k in range(1, n)]:
         pl.semaphore_signal(barrier, inc=1, device_id=target, device_id_type=pl.DeviceIdType.MESH)
@@ -214,7 +218,7 @@
             device_id=device, device_id_type=pl.DeviceIdType.MESH,
         )
 
-    kv_copy = remote(spatial.at[:, 1:3, 0], peer_kv, kv_sem.at[0], kv_sem.at[1], to_peer)
+    kv_copy = remote(spatial_in.at[:, 1:3, 0], peer_kv, kv_sem.at[0], kv_sem.at[1], to_peer)
     kv_copy.start()
 
     gathered = (out_all, qkv_all)
@@ -336,18 +340,19 @@
         whole = gathered[which].at[pl.ds(pl.multiple_of(me * sizes[which], 16), sizes[which])]
         own_copies.append(pltpu.make_async_copy(owned[which], whole, own_sem.at[which]))
         own_copies[-1].start()
+    stream_copy.start()
 
     events = []
     for distance in range(depths):
         if distance:
             events.append((2 * distance, line_step, (0, distance)))
-            events.append((14 + 4 * (distance - 1), line_step, (1, distance)))
+            events.append((4 * distance + 1, line_step, (1, distance)))
             events.append((2 * distance + 3, x_step, (0, distance, 0)))
-            events.append((16 + 5 * (distance - 1), x_step, (1, distance, 0)))
+            events.append((4 * distance + 6, x_step, (1, distance, 0)))
         events.append((2 * distance + 2.5, row_step, (0, distance)))
-        events.append((14.5 + 4.5 * distance, row_step, (1, distance)))
+        events.append((4 * distance + 5, row_step, (1, distance)))
         events.append((2 * distance + 5, x_step, (0, distance, 1)))
-        events.append((16.5 + 5 * distance, x_step, (1, distance, 1)))
+        events.append((4 * distance + 8, x_step, (1, distance, 1)))
     events.sort(key=lambda event: event[0])
 
     def serve(until):
@@ -360,6 +365,7 @@
             events.remove(event)
             event[1](*event[2])
 
+    spatial_copy.wait()
     kv_copy.wait_recv()
     tiles = LaneTiles(heads)
     for head in range(heads):
@@ -378,6 +384,7 @@
     serve_all(0)
     all_here(0)
     own_copies[0].wait()
+    stream_copy.wait()
 
     @pl.loop(0, width // TILE)
     def _(index):
@@ -418,7 +425,10 @@
                 rows_send.at[theirs], rows_recv.at[mine], row_send_sem.at[k], row_recv_sem.at[k], {"frame": frame}
             ))
             row_copies[-1].start()
-
+        serve(18 + k)
+
+    residual_copy = pltpu.make_async_copy(residual, residual_out, in_sem.at[2])
+    residual_copy.start()
     serve_all(1)
     all_here(1)
     own_copies[1].wait()
@@ -475,6 +485,7 @@
                     copy.start()
                     pieces[chunk, k] = copy
 
+    residual_copy.wait()
     kv_copy.wait_send()
     for which in (0, 1):
         all_sent(which)
@@ -488,13 +499,14 @@
         arrives(returned.at[chunk, source], back_recv_sem.at[chunk, k]).wait_recv()
 
 
-def finish_kernel(residual, returned, residual_out, temporal_out, blocks, temporal, sem):
+def finish_kernel(residual, returned, residual_out, temporal_out, blocks, held, temporal, sem):
     chunks, n, rows, tile = returned.shape
     part = rows // 2
     arrivals = [pltpu.make_async_copy(returned.at[c], blocks.at[c], sem.at[c]) for c in range(chunks)]
-    leaving = [pltpu.make_async_copy(residual.at[t], residual_out.at[t], sem.at[2 * chunks + t]) for t in (0, 1)]
-    for copy in arrivals + leaving:
+    passing = [pltpu.make_async_copy(residual.at[t], held.at[t], sem.at[2 * chunks + t]) for t in (0, 1)]
+    for copy in arrivals + passing:
         copy.start()
+    leaving = []
     for chunk in range(chunks):
         arrivals[chunk].wait()
         for f in range(n):
@@ -508,6 +520,12 @@
             temporal.at[:, :, :, columns], temporal_out.at[:, :, :, columns], sem.at[chunks + chunk]
         ))
         leaving[-1].start()
+        if chunk < 2:
+            passing[chunk].wait()
+            leaving.append(pltpu.make_async_copy(
+                held.at[chunk], residual_out.at[chunk], sem.at[2 * chunks + 2 + chunk]
+            ))
+            leaving[-1].start()
     for copy in leaving:
         copy.wait()
 
@@ -520,15 +538,20 @@
     bf16, f32 = jnp.bfloat16, jnp.float32
     dma = pltpu.SemaphoreType.DMA
     vmem = pl.BlockSpec(memory_space=pltpu.VMEM)
+    anywhere = pl.BlockSpec(memory_space=pl.ANY)
     residual, returned = pl.pallas_call(
         functools.partial(fused_kernel, n),
         out_shape=(
             jax.ShapeDtypeStruct(stream.shape, f32),
             jax.ShapeDtypeStruct((chunks, n, 2 * part, TILE), bf16),
         ),
-        in_specs=[vmem] * 5,
-        out_specs=(vmem, vmem),
+        in_specs=[anywhere] * 4 + [vmem],
+        out_specs=(anywhere, vmem),
         scratch_shapes=[
+            pltpu.VMEM(spatial_qkv.shape, bf16),
+            pltpu.VMEM(stream.shape, bf16),
+            pltpu.VMEM(stream.shape, f32),
+            dma((3,)),
             pltpu.VMEM((2, 2, places, width), bf16),
             pltpu.VMEM((width, width), bf16),
             pltpu.VMEM((3 * width, width), bf16),
@@ -546,10 +569,13 @@
     return tuple(pl.pallas_call(
         finish_kernel,
         out_shape=(jax.ShapeDtypeStruct(stream.shape, f32),) * 2,
-        in_specs=[pl.BlockSpec(memory_space=pl.ANY)] * 2,
-        out_specs=(pl.BlockSpec(memory_space=pl.ANY),) * 2,
+        in_specs=[anywhere] * 2,
+        out_specs=(anywhere,) * 2,
         scratch_shapes=[
-            pltpu.VMEM((chunks, n, 2 * part, TILE), bf16), pltpu.VMEM(stream.shape, f32), dma((2 * chunks + 2,))
+            pltpu.VMEM((chunks, n, 2 * part, TILE), bf16),
+            pltpu.VMEM(stream.shape, f32),
+            pltpu.VMEM(stream.shape, f32),
+            dma((2 * chunks + 4,)),
         ],
         compiler_params=pltpu.CompilerParams(vmem_limit_bytes=56 * 1024 * 1024),
     )(residual, returned))
@@ -566,6 +592,7 @@
         and (places // n) % 8 == 0
         and places % 16 == 0
         and width % TILE == 0
+        and width >= 2 * TILE
         and width % HEAD_DIM == 0
         and out_columns % 48 == 0
         and qkv_columns % 48 == 0

time: 161 us -> 103 us (0.64)
  Pallas kernels: 157 us -> 99.6 us
    pallas_call x1, Pallas kernels: 54.8 us -> 3.12 us  [per_device_fused(): pl.pallas_call(finish_kernel, out_shape=(jax.ShapeDtypeStruct(stream.shap...]
    pallas_call x1, Pallas kernels: 102 us -> 96.5 us  [per_device_fused(): pl.pallas_call(functools.partial(fused_kernel, n), out_shape=(jax.ShapeDt...]
where the time goes in v4:
time: 103 us
  Pallas kernels  99.6 us (97%)
  between operations  1.47 us (1%)
    pallas_call x1, Pallas kernels, per_device_fused(): pl.pallas_call(functools.partial(fused_kernel, n), out_shape=(jax.ShapeDt...  96.5 us
    pallas_call x1, Pallas kernels, per_device_fused(): pl.pallas_call(finish_kernel, out_shape=(jax.ShapeDtypeStruct(stream.shap...  3.12 us

profile of v4, /device:TPU:0, one launch (start us, length us, event | category | flops | bytes accessed | tf_op | source)
XLA Modules:
  0.0 102.6 jit_solution(14995762543528027654)
XLA Ops:
  1.3 0.1 multiply_sine_fusion
  1.4 0.8 fusion.5
  2.2 0.6 pad_maximum_fusion.mod
  2.9 96.5 %shard_map.77 = (f32[2,1,192,1152]{3,2,1,0:T(8,128)}, bf16[3,8,48,384]{3,2,1,0:T(8,128)(2,1)}) custom-call(bf16[2,3,1,192,1152]{4,3,2,1,0:T(8,128)(2,1)} %spatial_in.1, bf16[2,1,192,1152]{3,2,1,0:T(8,128)(2,1)} %stream_in.1, bf16[144,1152]{1,0:T(8,128)(2,1)} %bitcast.20, bf16[432,1152]{1,0:T(8,128)(2,1)} %bitcast.19, f32[6,1152]{1,0:T(8,128)} %pad_maximum_fusion.mod), custom_call_target="tpu_custom_call" | custom-call | tf_op jit(solution)/shard_map/pallas_call | solution.py:542
  99.3 3.1 %shard_map.78 = (f32[2,1,192,1152]{3,2,1,0:T(8,128)}, f32[2,1,192,1152]{3,2,1,0:T(8,128)}) custom-call(f32[2,1,192,1152]{3,2,1,0:T(8,128)} %get-tuple-element.4.residual, bf16[3,8,48,384]{3,2,1,0:T(8,128)(2,1)} %get-tuple-element.5.returned), custom_call_target="tpu_custom_call" | custom-call | tf_op jit(solution)/shard_map/pallas_call | solution.py:569
  (2 shorter events, 0.0 us)

commit v5 on v4

--- a/solution.py
+++ b/solution.py
@@ -347,12 +347,12 @@
         if distance:
             events.append((2 * distance, line_step, (0, distance)))
             events.append((4 * distance + 1, line_step, (1, distance)))
-            events.append((2 * distance + 3, x_step, (0, distance, 0)))
-            events.append((4 * distance + 6, x_step, (1, distance, 0)))
+            events.append((14 + distance / 8, x_step, (0, distance, 0)))
+            events.append((40 + 2 * distance, x_step, (1, distance, 0)))
         events.append((2 * distance + 2.5, row_step, (0, distance)))
-        events.append((4 * distance + 5, row_step, (1, distance)))
-        events.append((2 * distance + 5, x_step, (0, distance, 1)))
-        events.append((4 * distance + 8, x_step, (1, distance, 1)))
+        events.append((4 * distance + 5 if distance < 2 else 30 + distance, row_step, (1, distance)))
+        events.append((15 + distance / 8, x_step, (0, distance, 1)))
+        events.append((41 + 2 * distance, x_step, (1, distance, 1)))
     events.sort(key=lambda event: event[0])
 
     def serve(until):

time: 103 us -> 102 us (level)
  no operation moved by 1% of the time
where the time goes in v5:
time: 102 us
  Pallas kernels  99 us (97%)
  between operations  1.47 us (1%)
    pallas_call x1, Pallas kernels, per_device_fused(): pl.pallas_call(functools.partial(fused_kernel, n), out_shape=(jax.ShapeDt...  95.9 us
    pallas_call x1, Pallas kernels, per_device_fused(): pl.pallas_call(finish_kernel, out_shape=(jax.ShapeDtypeStruct(stream.shap...  3.12 us

profile of v5, /device:TPU:0, one launch (start us, length us, event | category | flops | bytes accessed | tf_op | source)
XLA Modules:
  0.0 102.0 jit_solution(15824755921841189251)
XLA Ops:
  1.3 0.1 multiply_sine_fusion
  1.4 0.8 fusion.5
  2.2 0.6 pad_maximum_fusion.mod
  2.9 95.9 %shard_map.77 = (f32[2,1,192,1152]{3,2,1,0:T(8,128)}, bf16[3,8,48,384]{3,2,1,0:T(8,128)(2,1)}) custom-call(bf16[2,3,1,192,1152]{4,3,2,1,0:T(8,128)(2,1)} %spatial_in.1, bf16[2,1,192,1152]{3,2,1,0:T(8,128)(2,1)} %stream_in.1, bf16[144,1152]{1,0:T(8,128)(2,1)} %bitcast.20, bf16[432,1152]{1,0:T(8,128)(2,1)} %bitcast.19, f32[6,1152]{1,0:T(8,128)} %pad_maximum_fusion.mod), custom_call_target="tpu_custom_call" | custom-call | tf_op jit(solution)/shard_map/pallas_call | solution.py:542
  98.8 3.1 %shard_map.78 = (f32[2,1,192,1152]{3,2,1,0:T(8,128)}, f32[2,1,192,1152]{3,2,1,0:T(8,128)}) custom-call(f32[2,1,192,1152]{3,2,1,0:T(8,128)} %get-tuple-element.4.residual, bf16[3,8,48,384]{3,2,1,0:T(8,128)(2,1)} %get-tuple-element.5.returned), custom_call_target="tpu_custom_call" | custom-call | tf_op jit(solution)/shard_map/pallas_call | solution.py:569
  (2 shorter events, 0.0 us)

commit v6 on v5

--- a/solution.py
+++ b/solution.py
@@ -350,7 +350,7 @@
             events.append((14 + distance / 8, x_step, (0, distance, 0)))
             events.append((40 + 2 * distance, x_step, (1, distance, 0)))
         events.append((2 * distance + 2.5, row_step, (0, distance)))
-        events.append((4 * distance + 5 if distance < 2 else 30 + distance, row_step, (1, distance)))
+        events.append((4 * distance + 5, row_step, (1, distance)))
         events.append((15 + distance / 8, x_step, (0, distance, 1)))
         events.append((41 + 2 * distance, x_step, (1, distance, 1)))
     events.sort(key=lambda event: event[0])

time: 102 us -> 105 us (1.029); the launches traced: 102 us -> 103 us
  no operation moved by 1% of the time
where the time goes in v6:
time: 105 us; the launch traced here: 103 us
  Pallas kernels  99.9 us (95%)
  between operations  1.47 us (1%)
    pallas_call x1, Pallas kernels, per_device_fused(): pl.pallas_call(functools.partial(fused_kernel, n), out_shape=(jax.ShapeDt...  96.8 us
    pallas_call x1, Pallas kernels, per_device_fused(): pl.pallas_call(finish_kernel, out_shape=(jax.ShapeDtypeStruct(stream.shap...  3.12 us

profile of v6, /device:TPU:0, one launch (start us, length us, event | category | flops | bytes accessed | tf_op | source)
XLA Modules:
  0.0 102.9 jit_solution(7106414133635873921)
XLA Ops:
  1.3 0.1 multiply_sine_fusion
  1.4 0.8 fusion.5
  2.2 0.6 pad_maximum_fusion.mod
  2.9 96.8 %shard_map.77 = (f32[2,1,192,1152]{3,2,1,0:T(8,128)}, bf16[3,8,48,384]{3,2,1,0:T(8,128)(2,1)}) custom-call(bf16[2,3,1,192,1152]{4,3,2,1,0:T(8,128)(2,1)} %spatial_in.1, bf16[2,1,192,1152]{3,2,1,0:T(8,128)(2,1)} %stream_in.1, bf16[144,1152]{1,0:T(8,128)(2,1)} %bitcast.20, bf16[432,1152]{1,0:T(8,128)(2,1)} %bitcast.19, f32[6,1152]{1,0:T(8,128)} %pad_maximum_fusion.mod), custom_call_target="tpu_custom_call" | custom-call | tf_op jit(solution)/shard_map/pallas_call | solution.py:542
  99.6 3.1 %shard_map.78 = (f32[2,1,192,1152]{3,2,1,0:T(8,128)}, f32[2,1,192,1152]{3,2,1,0:T(8,128)}) custom-call(f32[2,1,192,1152]{3,2,1,0:T(8,128)} %get-tuple-element.4.residual, bf16[3,8,48,384]{3,2,1,0:T(8,128)(2,1)} %get-tuple-element.5.returned), custom_call_target="tpu_custom_call" | custom-call | tf_op jit(solution)/shard_map/pallas_call | solution.py:569
  (2 shorter events, 0.0 us)
